TPU v7x, 32 devices: a whole 2x2x4 slice. The times are simulated.
32 devices in a mesh: occ: 16 (over z, y, x), aux: 2 (over core).
Axes of the slice: x: 2, y: 2, z: 4, core: 2. Of those that a mesh axis runs over, the one named last changes fastest.
Arguments:
- b_rows: bfloat16 [12288, 2048], P('aux', 'occ'), may hold values from -0.5 to 0.5
- b_cols: bfloat16 [12288, 8192], P('aux', 'occ'), may hold values from -0.5 to 0.5
- eps_occ: float32 [32], replicated, may hold values from -1.5 to -0.3
- eps_va: float32 [64], replicated, may hold values from 0.2 to 2
- eps_vb: float32 [256], replicated, may hold values from 0.2 to 2
Outputs:
- gamma: float32 [12288, 2048], P('aux', 'occ')
All inputs are finite; a program needn't handle non-finite values.
Results may differ from a plain program's by a relative error of at most 0.0027.
Values may be sent and summed in bfloat16 or wider, within the bound.
A program may use at most 64 MiB of HBM per device.

v0:
```python
import jax
import jax.numpy as jnp
from jax import lax
from jax.sharding import PartitionSpec as P

spin_scale = 1.3


def passed_along(value, axis, by):
    size = lax.axis_size(axis)
    return lax.ppermute(value, axis, [(i, (i + by) % size) for i in range(size)])


def partial_integrals(left_block, right_block):
    return lax.dot_general(
        left_block, right_block, (((0,), (0,)), ((), ())), preferred_element_type=jnp.float32
    )


def amplitudes(summed, row_energy, col_energy):
    return (spin_scale * summed / (row_energy[:, None] + col_energy[None, :])).astype(jnp.bfloat16)


def contribution(right_block, amplitude):
    return lax.dot_general(
        right_block, amplitude, (((1,), (1,)), ((), ())), preferred_element_type=jnp.float32
    )


def per_device(b_rows, b_cols, eps_occ, eps_va, eps_vb):
    per_block = b_rows.shape[1] // eps_va.shape[0]
    cycle_size = lax.axis_size("occ")
    position = lax.axis_index("occ")

    def energy(offset, virt_energy):
        which = (position + offset) % cycle_size
        occ_energy = lax.dynamic_slice_in_dim(eps_occ, which * per_block, per_block)
        return (virt_energy[None, :] - occ_energy[:, None]).reshape(-1)

    right_list = [b_cols]
    moving = b_cols
    for hop_index in range(2):
        moving = passed_along(moving, "occ", 1)
        right_list.append(moving)
    left_list = [b_rows, b_rows, b_rows]
    own_rows = energy(0, eps_va)
    row_list = [own_rows, own_rows, own_rows]
    col_list = [energy(0, eps_vb), energy(-1, eps_vb), energy(-2, eps_vb)]
    partials = []
    for index in range(3):
        partials.append(partial_integrals(left_list[index], right_list[index]))
    summed_list = []
    for index in range(3):
        summed_list.append(lax.psum(partials[index], "aux"))
    pieces = []
    for index in range(3):
        amplitude = amplitudes(summed_list[index], row_list[index], col_list[index])
        pieces.append(contribution(right_list[index], amplitude))
    gamma = pieces[0] + pieces[1] + pieces[2]
    return gamma


def solution(mesh):
    return jax.shard_map(
        per_device,
        mesh=mesh,
        in_specs=(P("aux", "occ"), P("aux", "occ"), P(), P(), P()),
        out_specs=P("aux", "occ"),
        check_vma=False,
    )
```

profile of v0, /device:TPU:1, one launch (start us, length us, event | category | flops | bytes accessed | tf_op | source)
XLA Modules:
  0.0 333.4 jit_solution(12476438801887291550)
XLA Ops:
  6.5 0.0 copy-start
  6.5 0.0 all-reduce.3.cloned.1.call-start
  6.5 2.0 collective-permute-start
  8.6 139.4 %collective-permute-done = bf16[6144,512]{1,0:T(8,128)(2,1)S(1)} collective-permute-done((bf16[6144,512]{1,0:T(8,128)(2,1)}, bf16[6144,512]{1,0:T(8,128)(2,1)S(1)}, u32[]{:S(2)}, u32[]{:S(2)}) %collective-permute-start) | collective-permute-done | bytes 6291488 | tf_op jit(solution)/shard_map/ppermute | solution.py:11
  148.0 0.0 copy-start.1
  148.0 0.0 collective-permute-start.1
  148.0 0.0 copy-done
  148.0 6.8 %fusion.15 = f32[128,512]{1,0:T(8,128)} fusion(bf16[6144,128]{1,0:T(8,128)(2,1)S(1)} %copy-done, bf16[6144,512]{1,0:T(8,128)(2,1)} %param.6), kind=kOutput, calls=%fused_computation.24 | convolution fusion | flops 805306368 | bytes 8126464 | tf_op jit(solution)/shard_map/dot_general | solution.py:15
  154.8 1.7 fusion.16
  156.6 0.0 copy-done.1
  156.6 0.0 copy-start.6
  156.6 0.0 copy-start.8
  156.6 0.0 copy-start.7
  156.6 130.8 %collective-permute-done.1 = bf16[6144,512]{1,0:T(8,128)(2,1)S(1)} collective-permute-done((bf16[6144,512]{1,0:T(8,128)(2,1)S(1)}, bf16[6144,512]{1,0:T(8,128)(2,1)S(1)}, u32[]{:S(2)}, u32[]{:S(2)}) %collective-permute-start.1) | collective-permute-done | bytes 6291488 | tf_op jit(solution)/shard_map/ppermute | solution.py:11
  287.4 0.0 copy-start.2
  287.4 2.6 copy-done.2
  290.0 1.7 fusion.17
  291.8 0.0 all-reduce.3.cloned.1.call-update
  291.8 0.0 copy-done.6
  291.8 0.1 fusion.14
  291.9 0.0 copy-done.8
  291.9 0.1 broadcast_subtract_fusion
  292.0 0.1 sub.79
  292.1 0.0 copy-done.7
  292.1 0.1 subtract_bitcast_fusion
  292.2 16.8 %all-reduce.3.cloned.1.call-done = (f32[128,512]{1,0:T(8,128)}, f32[128,512]{1,0:T(8,128)}, f32[128,512]{1,0:T(8,128)}) async-done(((f32[128,512]{1,0:T(8,128)}, f32[128,512]{1,0:T(8,128)}, f32[128,512]{1,0:T(8,128)}), (f32[128,512]{1,0:T(8,128)}, f32[128,512]{1,0:T(8,128)}, f32[128,512]{1,0:T(8,128)})) %all-reduce.3.cloned.1.call-update) | async-done | bytes 786448 | tf_op jit(solution)/shard_map/psum | solution.py:54
  308.9 0.0 copy-start.5
  308.9 5.1 %fusion.1 = f32[128,6144]{1,0:T(8,128)S(1)} fusion(bf16[6144,512]{1,0:T(8,128)(2,1)} %param.6, f32[128,512]{1,0:T(8,128)} %get-tuple-element.5, f32[512]{0:T(512)S(1)} %bitcast.20, f32[128]{0:T(128)S(1)} %sub.79), kind=kOutput, calls=%fused_computation.6 | convolution fusion | flops 805568512 | bytes 9701888 | tf_op jit(solution)/shard_map/dot_general | solution.py:25
  314.0 0.0 copy-done.5
  314.0 0.0 copy-start.3
  314.1 0.0 copy-start.4
  314.1 5.2 %convolution_add_fusion.1 = f32[128,6144]{1,0:T(8,128)S(1)} fusion(f32[128,6144]{1,0:T(8,128)S(1)} %fusion.1, bf16[6144,512]{1,0:T(8,128)(2,1)} %copy-done.1, f32[128,512]{1,0:T(8,128)S(1)} %copy-done.5, f32[512]{0:T(512)S(1)} %bitcast.22, f32[128]{0:T(128)S(1)} %sub.79), kind=kOutput, calls=%fused_computation.2 | convolution fusion | flops 806354944 | bytes 12847616 | tf_op jit(solution)/shard_map/dot_general | solution.py:25
  319.2 0.0 copy-done.3
  319.2 0.0 copy-done.4
  319.2 3.8 %fusion = f32[6144,128]{0,1:T(8,128)} fusion(f32[128,6144]{1,0:T(8,128)S(1)} %convolution_add_fusion.1, bf16[6144,512]{1,0:T(8,128)(2,1)S(1)} %copy-done.3, f32[128,512]{1,0:T(8,128)S(1)} %copy-done.4, f32[512]{0:T(512)S(1)} %bitcast.21, f32[128]{0:T(128)S(1)} %sub.79), kind=kOutput, calls=%fused_computation.1 | convolution fusion | flops 806354944 | bytes 12847616 | tf_op jit(solution)/shard_map/dot_general | solution.py:25
  323.1 3.5 %copy.6 = f32[6144,128]{1,0:T(8,128)} copy(f32[6144,128]{0,1:T(8,128)} %fusion) | data formatting | bytes 6291456 | tf_op jit(solution)/shard_map/add | solution.py:59
  (3 shorter events, 0.0 us)
Async XLA Ops:
  6.5 141.5 %copy-start = (bf16[6144,128]{1,0:T(8,128)(2,1)S(1)}, bf16[6144,128]{1,0:T(8,128)(2,1)}, u32[]{:S(2)}) copy-start(bf16[6144,128]{1,0:T(8,128)(2,1)} %param.5) | copy-start | bytes 4718596
  6.5 302.4 %all-reduce.3.cloned.1.call-start = ((), (), s32[]{:S(2)}) async-start(), calls=%async_computation | async-start | bytes 1572864 | tf_op jit(solution)/shard_map/psum | solution.py:54
  6.5 141.5 %collective-permute-start = (bf16[6144,512]{1,0:T(8,128)(2,1)}, bf16[6144,512]{1,0:T(8,128)(2,1)S(1)}, u32[]{:S(2)}, u32[]{:S(2)}) collective-permute-start(bf16[6144,512]{1,0:T(8,128)(2,1)} %param.6), channel_id=1, source_target_pairs={{0,2},{2,4},{4,6},{6,8},{8,10},{10,12},{12,14},{14,16},{16,18},{18... | collective-permute-start | bytes 18874376 | tf_op jit(solution)/shard_map/ppermute | solution.py:11
  148.0 8.5 %copy-start.1 = (bf16[6144,512]{1,0:T(8,128)(2,1)}, bf16[6144,512]{1,0:T(8,128)(2,1)S(1)}, u32[]{:S(2)}) copy-start(bf16[6144,512]{1,0:T(8,128)(2,1)S(1)} %collective-permute-done) | copy-start | bytes 18874372
  148.0 139.4 %collective-permute-start.1 = (bf16[6144,512]{1,0:T(8,128)(2,1)S(1)}, bf16[6144,512]{1,0:T(8,128)(2,1)S(1)}, u32[]{:S(2)}, u32[]{:S(2)}) collective-permute-start(bf16[6144,512]{1,0:T(8,128)(2,1)S(1)} %collective-permute-done), channel_id=1, source_target_pairs={{0,2},{2,4},{4,6},{6,8},{8,10},{10,12},{12,14},{14,16},{16,18},{18... | collective-permute-start | bytes 18874376 | tf_op jit(solution)/shard_map/ppermute | solution.py:11
  156.6 135.3 %copy-start.6 = (f32[32]{0:T(128)S(1)}, f32[32]{0:T(128)}, u32[]{:S(2)}) copy-start(f32[32]{0:T(128)} %param.7) | copy-start | bytes 388
  156.6 135.4 %copy-start.8 = (f32[64]{0:T(128)S(1)}, f32[64]{0:T(128)}, u32[]{:S(2)}) copy-start(f32[64]{0:T(128)} %param.8) | copy-start | bytes 772
  156.6 135.5 %copy-start.7 = (f32[256]{0:T(256)S(1)}, f32[256]{0:T(256)}, u32[]{:S(2)}) copy-start(f32[256]{0:T(256)} %param.9) | copy-start | bytes 3076
  287.4 2.6 copy-start.2
  308.9 5.1 %copy-start.5 = (f32[128,512]{1,0:T(8,128)S(1)}, f32[128,512]{1,0:T(8,128)}, u32[]{:S(2)}) copy-start(f32[128,512]{1,0:T(8,128)} %get-tuple-element.6) | copy-start | bytes 786436
  314.0 5.2 %copy-start.3 = (bf16[6144,512]{1,0:T(8,128)(2,1)S(1)}, bf16[6144,512]{1,0:T(8,128)(2,1)}, u32[]{:S(2)}) copy-start(bf16[6144,512]{1,0:T(8,128)(2,1)} %copy-done.2) | copy-start | bytes 18874372
  314.1 5.2 %copy-start.4 = (f32[128,512]{1,0:T(8,128)S(1)}, f32[128,512]{1,0:T(8,128)}, u32[]{:S(2)}) copy-start(f32[128,512]{1,0:T(8,128)} %get-tuple-element.7) | copy-start | bytes 786436
Sparse Core Ops, SparseCore 0:
  291.9 16.9 all-reduce.2
where the time goes:
time: 334 us; the launch traced here: 333 us
  waiting for transfers between devices  287 us (86%)
  matrix products  24.3 us (7%)
  between operations  13.5 us (4%)
  local copies, waits for them, and re-layouts  6.38 us (2%)
    ppermute x2, waiting for transfers between devices, passed_along(): lax.ppermute(value, axis, [(i, (i + by) % size) for i in range(size)])  270 us
    psum x1, waiting for transfers between devices, per_device(): summed_list.append(lax.psum(partials[index], 'aux'))  16.8 us
    dot_general x3, matrix products, contribution(): lax.dot_general(right_block, amplitude, (((1,), (1,)), ((), ())), preferr...  14.1 us
    dot_general x3, matrix products, partial_integrals(): lax.dot_general(left_block, right_block, (((0,), (0,)), ((), ())), prefer...  10.2 us
  transfers between devices with their start and end apart: 3, of which 3 were waited for; matrix products, arithmetic and copies ran while one was open for 3% of the time, Pallas kernels for 0%

commit v1 on v0

v1 whole, which is shorter than its diff:
```python
import functools

import jax
import jax.numpy as jnp
from jax import lax
from jax.experimental import pallas as pl
from jax.experimental.pallas import tpu as pltpu
from jax.sharding import PartitionSpec as P

spin_scale = 1.3
MESH = pl.DeviceIdType.MESH
CHUNKS = 16


def kernel(
    n, n_aux, chunks,
    rows_hbm, cols_hbm, occ_ref, va_ref, vb_ref, out_hbm,
    cols, own, rows1, rows2, v, v_in, factor, amp, g1_out, g2_out, g1_in, g2_in, g2, total,
    cols_sem, own_sem, out_sem, rows_send, rows_recv, g_send, g_recv, v_send, v_recv,
):
    p = lax.axis_index("occ")
    a = lax.axis_index("aux")
    depth, width = rows_hbm.shape
    wide = cols_hbm.shape[1]
    ch = depth // chunks
    two_down = lax.rem(p + (n - 2), n)
    two_up = lax.rem(p + 2, n)
    odd = lax.rem(p, 2)
    pair = p + 1 - 2 * odd

    def part(c):
        return pl.ds(pl.multiple_of(c * ch, ch), ch)

    def rows_two(c):
        return pltpu.make_async_remote_copy(
            src_ref=rows_hbm.at[part(c)], dst_ref=rows2.at[part(c)],
            send_sem=rows_send.at[1, c], recv_sem=rows_recv.at[1, c],
            device_id=(two_down, a), device_id_type=MESH)

    def rows_one_odd(c):
        return pltpu.make_async_remote_copy(
            src_ref=rows_hbm.at[part(c)], dst_ref=rows1.at[part(c)],
            send_sem=rows_send.at[0, c], recv_sem=rows_recv.at[0, c],
            device_id=(pair, a), device_id_type=MESH)

    def rows_one_even(c):
        return pltpu.make_async_remote_copy(
            src_ref=rows2.at[part(c)], dst_ref=rows1.at[part(c)],
            send_sem=rows_send.at[0, c], recv_sem=rows_recv.at[0, c],
            device_id=(pair, a), device_id_type=MESH)

    def gamma_one(c):
        return pltpu.make_async_remote_copy(
            src_ref=g1_out.at[part(c)], dst_ref=g1_in.at[part(c)],
            send_sem=g_send.at[0, c], recv_sem=g_recv.at[0, c],
            device_id=(pair, a), device_id_type=MESH)

    def gamma_two(c):
        return pltpu.make_async_remote_copy(
            src_ref=g2_out.at[part(c)], dst_ref=g2_in.at[part(c)],
            send_sem=g_send.at[1, c], recv_sem=g_recv.at[1, c],
            device_id=(two_up, a), device_id_type=MESH)

    def v_copy(s, d):
        return pltpu.make_async_remote_copy(
            src_ref=v.at[s], dst_ref=v_in.at[d - 1, s],
            send_sem=v_send.at[d - 1, s], recv_sem=v_recv.at[d - 1, s],
            device_id=(p, lax.rem(a + d, n_aux)), device_id_type=MESH)

    def cols_copy(c):
        return pltpu.make_async_copy(cols_hbm.at[part(c)], cols.at[part(c)], cols_sem.at[c])

    def own_copy(c):
        return pltpu.make_async_copy(rows_hbm.at[part(c)], own.at[part(c)], own_sem.at[c])

    def out_copy(c):
        return pltpu.make_async_copy(total.at[part(c)], out_hbm.at[part(c)], out_sem.at[c])

    barrier = pltpu.get_barrier_semaphore()
    peers = [(two_down, a), (two_up, a), (pair, a)]
    peers += [(p, lax.rem(a + d, n_aux)) for d in range(1, n_aux)]
    for peer in peers:
        pl.semaphore_signal(barrier, inc=1, device_id=peer, device_id_type=MESH)

    @pl.loop(0, chunks)
    def _(c):
        cols_copy(c).start()
        own_copy(c).start()

    pl.semaphore_wait(barrier, len(peers))

    @pl.loop(0, chunks)
    def _(c):
        rows_two(c).start()

        @pl.when(odd == 1)
        def _():
            rows_one_odd(c).start()

    per_block = width // va_ref.shape[1]
    col = jnp.concatenate([vb_ref[...] - occ_ref[p * per_block + i] for i in range(per_block)], axis=1)
    for s in range(3):
        which = lax.rem(p + s, n)
        row = jnp.concatenate([va_ref[...] - occ_ref[which * per_block + i] for i in range(per_block)], axis=1)
        row = jnp.broadcast_to(row, (width, width)).T
        for at in range(0, wide, width):
            factor[s, :, at:at + width] = spin_scale / (row + col[:, at:at + width])
    v[...] = jnp.zeros_like(v)

    def integrals(s, left, c):
        v[s] += lax.dot_general(
            left[part(c), :], cols[part(c), :], (((0,), (0,)), ((), ())),
            preferred_element_type=jnp.float32)

    @pl.loop(0, chunks)
    def _(c):
        cols_copy(c).wait()
        own_copy(c).wait()
        integrals(0, own, c)
        rows_two(c).wait_recv()

        @pl.when(odd == 0)
        def _():
            rows_one_even(c).start()

        integrals(2, rows2, c)
        rows_one_odd(c).wait_recv()
        integrals(1, rows1, c)

    for s in (1, 2, 0):
        for d in range(1, n_aux):
            v_copy(s, d).start()

    def amplitude(s):
        summed = v[s]
        for d in range(1, n_aux):
            v_copy(s, d).wait_recv()
            summed += v_in[d - 1, s]
        amp[s * width:(s + 1) * width, :] = (summed * factor[s]).astype(jnp.bfloat16)

    def pieces(c, first, last):
        return lax.dot_general(
            cols[part(c), :], amp[first * width:last * width, :], (((1,), (1,)), ((), ())),
            preferred_element_type=jnp.float32)

    amplitude(1)
    amplitude(2)

    @pl.loop(0, chunks)
    def _(c):
        both = pieces(c, 1, 3)
        g1_out[part(c), :] = both[:, :width].astype(jnp.bfloat16)
        gamma_one(c).start()

        @pl.when(odd == 1)
        def _():
            g2_out[part(c), :] = both[:, width:].astype(jnp.bfloat16)
            gamma_two(c).start()

        @pl.when(odd == 0)
        def _():
            g2[part(c), :] = both[:, width:]

    amplitude(0)

    @pl.loop(0, chunks)
    def _(c):
        @pl.when(odd == 0)
        def _():
            gamma_one(c).wait_recv()
            g2_out[part(c), :] = (g2[part(c), :] + g1_in[part(c), :].astype(jnp.float32)).astype(jnp.bfloat16)
            gamma_two(c).start()

        total[part(c), :] = pieces(c, 0, 1)

    @pl.loop(0, chunks)
    def _(c):
        @pl.when(odd == 1)
        def _():
            gamma_one(c).wait_recv()
            total[part(c), :] += g1_in[part(c), :].astype(jnp.float32)

        gamma_two(c).wait_recv()
        total[part(c), :] += g2_in[part(c), :].astype(jnp.float32)
        out_copy(c).start()

    for s in range(3):
        for d in range(1, n_aux):
            v_copy(s, d).wait_send()

    @pl.loop(0, chunks)
    def _(c):
        rows_two(c).wait_send()
        rows_one_odd(c).wait_send()
        gamma_one(c).wait_send()
        gamma_two(c).wait_send()
        out_copy(c).wait()


def per_device(n, n_aux, b_rows, b_cols, eps_occ, eps_va, eps_vb):
    depth, width = b_rows.shape
    wide = b_cols.shape[1]
    chunks = CHUNKS
    f32, bf16 = jnp.float32, jnp.bfloat16
    dma = pltpu.SemaphoreType.DMA
    return pl.pallas_call(
        functools.partial(kernel, n, n_aux, chunks),
        out_shape=jax.ShapeDtypeStruct((depth, width), f32),
        in_specs=[
            pl.BlockSpec(memory_space=pl.ANY),
            pl.BlockSpec(memory_space=pl.ANY),
            pl.BlockSpec(memory_space=pltpu.SMEM),
            pl.BlockSpec(memory_space=pltpu.VMEM),
            pl.BlockSpec(memory_space=pltpu.VMEM),
        ],
        out_specs=pl.BlockSpec(memory_space=pl.ANY),
        scratch_shapes=[
            pltpu.VMEM((depth, wide), bf16),
            pltpu.VMEM((depth, width), bf16),
            pltpu.VMEM((depth, width), bf16),
            pltpu.VMEM((depth, width), bf16),
            pltpu.VMEM((3, width, wide), f32),
            pltpu.VMEM((n_aux - 1, 3, width, wide), f32),
            pltpu.VMEM((3, width, wide), f32),
            pltpu.VMEM((3 * width, wide), bf16),
            pltpu.VMEM((depth, width), bf16),
            pltpu.VMEM((depth, width), bf16),
            pltpu.VMEM((depth, width), bf16),
            pltpu.VMEM((depth, width), bf16),
            pltpu.VMEM((depth, width), f32),
            pltpu.VMEM((depth, width), f32),
            dma((chunks,)),
            dma((chunks,)),
            dma((chunks,)),
            dma((2, chunks)),
            dma((2, chunks)),
            dma((2, chunks)),
            dma((2, chunks)),
            dma((n_aux - 1, 3)),
            dma((n_aux - 1, 3)),
        ],
        compiler_params=pltpu.CompilerParams(
            collective_id=0, has_side_effects=True, vmem_limit_bytes=48 * 1024 * 1024),
        cost_estimate=pl.CostEstimate(
            flops=12 * depth * width * wide, bytes_accessed=2 * depth * (wide + 3 * width), transcendentals=0),
    )(b_rows, b_cols, eps_occ, eps_va[None, :], eps_vb[None, :])


def solution(mesh):
    return jax.shard_map(
        functools.partial(per_device, mesh.shape["occ"], mesh.shape["aux"]),
        mesh=mesh,
        in_specs=(P("aux", "occ"), P("aux", "occ"), P(), P(), P()),
        out_specs=P("aux", "occ"),
        check_vma=False,
    )
```

time: 334 us -> 96.2 us (0.29)
  waiting for transfers between devices: 287 us -> 0 us
  Pallas kernels: 0 us -> 90.9 us
  matrix products: 24.3 us -> 0 us
  between operations: 13.5 us -> 0.01 us
    ppermute x2 -> x0, waiting for transfers between devices: 270 us -> none  [passed_along(): lax.ppermute(value, axis, [(i, (i + by) % size) for i in range(size)])]
    pallas_call x0 -> x1, Pallas kernels: none -> 90.9 us  [per_device(): pl.pallas_call(functools.partial(kernel, n, n_aux, chunks), out_shape=jax...]
    dot_general x6 -> x0, matrix products: 24.3 us -> none  [the longest x3 14.1 us: contribution(): lax.dot_general(right_block, amplitude, (((1,), (1,)), ((), ())), preferr...]
    psum x1 -> x0, waiting for transfers between devices: 16.8 us -> none  [per_device(): summed_list.append(lax.psum(partials[index], 'aux'))]
    add x1 -> x0, local copies, waits for them, and re-layouts: 3.54 us -> none  [per_device(): gamma = pieces[0] + pieces[1] + pieces[2]]
  transfers between devices with their start and end apart: 3 -> 0, of which waited for: 3 -> 0; matrix products, arithmetic and copies ran while one was open for 3% -> 0% of each run, Pallas kernels for 0% -> 0%
where the time goes in v1:
time: 96.2 us; the launch traced here: 96 us
  Pallas kernels  90.9 us (94%)
  local copies, waits for them, and re-layouts  5.06 us (5%)
    pallas_call x1, Pallas kernels, per_device(): pl.pallas_call(functools.partial(kernel, n, n_aux, chunks), out_shape=jax...  90.9 us
    unnamed x9, local copies, waits for them, and re-layouts  5.06 us

profile of v1, /device:TPU:1, one launch (start us, length us, event | category | flops | bytes accessed | tf_op | source)
XLA Modules:
  0.0 96.0 jit_solution(12267325904979630644)
XLA Ops:
  0.0 0.0 copy-start
  0.0 1.4 %copy-done = bf16[6144,128]{1,0:T(8,128)(2,1)S(1)} copy-done((bf16[6144,128]{1,0:T(8,128)(2,1)S(1)}, bf16[6144,128]{1,0:T(8,128)(2,1)}, u32[]{:S(2)}) %copy-start) | copy-done | bytes 1572888
  1.4 0.0 copy-start.1
  1.4 0.7 copy-done.1
  2.1 0.0 copy-start.2
  2.1 0.7 copy-done.2
  2.7 0.0 copy-start.3
  2.7 0.7 copy-done.3
  3.4 90.9 %shard_map.55 = f32[6144,128]{1,0:T(8,128)S(1)} custom-call(bf16[6144,128]{1,0:T(8,128)(2,1)S(1)} %copy-done, bf16[6144,512]{1,0:T(8,128)(2,1)} %cols_hbm.1, f32[32]{0:T(128)S(1)} %copy-done.2, f32[1,64]{1,0:T(1,128)S(1)} %bitcast.3, f32[1,256]{1,0:T(1,128)S(1)} %bitcast.2), custom_call_target="tpu_custom_call" | custom-call | flops 4831838208 | bytes 11010048 | tf_op jit(solution)/shard_map/pallas_call | solution.py:206
  94.4 1.7 %copy.7 = f32[6144,128]{1,0:T(8,128)} copy(f32[6144,128]{1,0:T(8,128)S(1)} %shard_map.55) | data formatting | bytes 6291456
Async XLA Ops:
  0.0 1.4 %copy-start = (bf16[6144,128]{1,0:T(8,128)(2,1)S(1)}, bf16[6144,128]{1,0:T(8,128)(2,1)}, u32[]{:S(2)}) copy-start(bf16[6144,128]{1,0:T(8,128)(2,1)} %rows_hbm.1) | copy-start | bytes 4718596
  1.4 0.7 copy-start.1
  2.1 0.7 copy-start.2
  2.7 0.7 copy-start.3

commit v2 on v1

--- a/solution.py
+++ b/solution.py
@@ -14,9 +14,9 @@
 
 def kernel(
     n, n_aux, chunks,
-    rows_hbm, cols_hbm, occ_ref, va_ref, vb_ref, out_hbm,
-    cols, own, rows1, rows2, v, v_in, factor, amp, g1_out, g2_out, g1_in, g2_in, g2, total,
-    cols_sem, own_sem, out_sem, rows_send, rows_recv, g_send, g_recv, v_send, v_recv,
+    rows_hbm, cols_hbm, occ_hbm, va_hbm, vb_hbm, total,
+    cols, own, rows1, rows2, v, v_in, factor, amp, g1_out, g2_out, g1_in, g2_in, g2, occ_ref, va_ref, vb_ref,
+    energy_sem, cols_sem, own_sem, rows_send, rows_recv, g_send, g_recv, v_send, v_recv,
 ):
     p = lax.axis_index("occ")
     a = lax.axis_index("aux")
@@ -73,30 +73,35 @@
     def own_copy(c):
         return pltpu.make_async_copy(rows_hbm.at[part(c)], own.at[part(c)], own_sem.at[c])
 
-    def out_copy(c):
-        return pltpu.make_async_copy(total.at[part(c)], out_hbm.at[part(c)], out_sem.at[c])
-
     barrier = pltpu.get_barrier_semaphore()
     peers = [(two_down, a), (two_up, a), (pair, a)]
     peers += [(p, lax.rem(a + d, n_aux)) for d in range(1, n_aux)]
     for peer in peers:
         pl.semaphore_signal(barrier, inc=1, device_id=peer, device_id_type=MESH)
 
+    energies = [
+        pltpu.make_async_copy(src, dst, energy_sem.at[i])
+        for i, (src, dst) in enumerate([(occ_hbm, occ_ref), (va_hbm, va_ref), (vb_hbm, vb_ref)])
+    ]
+    for energy in energies:
+        energy.start()
+    pl.semaphore_wait(barrier, len(peers))
+
+    @pl.loop(0, chunks)
+    def _(c):
+        rows_two(c).start()
+
+        @pl.when(odd == 1)
+        def _():
+            rows_one_odd(c).start()
+
     @pl.loop(0, chunks)
     def _(c):
         cols_copy(c).start()
         own_copy(c).start()
 
-    pl.semaphore_wait(barrier, len(peers))
-
-    @pl.loop(0, chunks)
-    def _(c):
-        rows_two(c).start()
-
-        @pl.when(odd == 1)
-        def _():
-            rows_one_odd(c).start()
-
+    for energy in energies:
+        energy.wait()
     per_block = width // va_ref.shape[1]
     col = jnp.concatenate([vb_ref[...] - occ_ref[p * per_block + i] for i in range(per_block)], axis=1)
     for s in range(3):
@@ -182,7 +187,6 @@
 
         gamma_two(c).wait_recv()
         total[part(c), :] += g2_in[part(c), :].astype(jnp.float32)
-        out_copy(c).start()
 
     for s in range(3):
         for d in range(1, n_aux):
@@ -194,7 +198,6 @@
         rows_one_odd(c).wait_send()
         gamma_one(c).wait_send()
         gamma_two(c).wait_send()
-        out_copy(c).wait()
 
 
 def per_device(n, n_aux, b_rows, b_cols, eps_occ, eps_va, eps_vb):
@@ -207,13 +210,13 @@
         functools.partial(kernel, n, n_aux, chunks),
         out_shape=jax.ShapeDtypeStruct((depth, width), f32),
         in_specs=[
-            pl.BlockSpec(memory_space=pl.ANY),
-            pl.BlockSpec(memory_space=pl.ANY),
-            pl.BlockSpec(memory_space=pltpu.SMEM),
-            pl.BlockSpec(memory_space=pltpu.VMEM),
-            pl.BlockSpec(memory_space=pltpu.VMEM),
+            pl.BlockSpec(memory_space=pltpu.HBM),
+            pl.BlockSpec(memory_space=pltpu.HBM),
+            pl.BlockSpec(memory_space=pltpu.HBM),
+            pl.BlockSpec(memory_space=pltpu.HBM),
+            pl.BlockSpec(memory_space=pltpu.HBM),
         ],
-        out_specs=pl.BlockSpec(memory_space=pl.ANY),
+        out_specs=pl.BlockSpec(memory_space=pltpu.VMEM),
         scratch_shapes=[
             pltpu.VMEM((depth, wide), bf16),
             pltpu.VMEM((depth, width), bf16),
@@ -228,8 +231,10 @@
             pltpu.VMEM((depth, width), bf16),
             pltpu.VMEM((depth, width), bf16),
             pltpu.VMEM((depth, width), f32),
-            pltpu.VMEM((depth, width), f32),
-            dma((chunks,)),
+            pltpu.SMEM(eps_occ.shape, f32),
+            pltpu.VMEM((1, eps_va.shape[0]), f32),
+            pltpu.VMEM((1, eps_vb.shape[0]), f32),
+            dma((3,)),
             dma((chunks,)),
             dma((chunks,)),
             dma((2, chunks)),

time: 96.2 us -> 95.2 us (0.990)
    pallas_call x1, Pallas kernels: 90.9 us -> 90 us  [per_device(): pl.pallas_call(functools.partial(kernel, n, n_aux, chunks), out_shape=jax...]
where the time goes in v2:
time: 95.2 us; the launch traced here: 95.1 us
  Pallas kernels  90 us (95%)
  local copies, waits for them, and re-layouts  5.06 us (5%)
    pallas_call x1, Pallas kernels, per_device(): pl.pallas_call(functools.partial(kernel, n, n_aux, chunks), out_shape=jax...  90 us
    unnamed x9, local copies, waits for them, and re-layouts  5.06 us

profile of v2, /device:TPU:1, one launch (start us, length us, event | category | flops | bytes accessed | tf_op | source)
XLA Modules:
  0.0 95.1 jit_solution(5023052023994379858)
XLA Ops:
  0.0 0.0 copy-start
  0.0 1.4 %copy-done = bf16[6144,128]{1,0:T(8,128)(2,1)S(1)} copy-done((bf16[6144,128]{1,0:T(8,128)(2,1)S(1)}, bf16[6144,128]{1,0:T(8,128)(2,1)}, u32[]{:S(2)}) %copy-start) | copy-done | bytes 1572888
  1.4 0.0 copy-start.1
  1.4 0.7 copy-done.1
  2.1 0.0 copy-start.2
  2.1 0.7 copy-done.2
  2.7 0.0 copy-start.3
  2.7 0.7 copy-done.3
  3.4 90.0 %shard_map.55 = f32[6144,128]{1,0:T(8,128)S(1)} custom-call(bf16[6144,128]{1,0:T(8,128)(2,1)S(1)} %copy-done, bf16[6144,512]{1,0:T(8,128)(2,1)} %cols_hbm.1, f32[32]{0:T(128)S(1)} %copy-done.2, f32[1,64]{1,0:T(1,128)S(1)} %bitcast.3, f32[1,256]{1,0:T(1,128)S(1)} %bitcast.2), custom_call_target="tpu_custom_call" | custom-call | flops 4831838208 | bytes 11010048 | tf_op jit(solution)/shard_map/pallas_call | solution.py:209
  93.4 1.7 %copy.7 = f32[6144,128]{1,0:T(8,128)} copy(f32[6144,128]{1,0:T(8,128)S(1)} %shard_map.55) | data formatting | bytes 6291456
Async XLA Ops:
  0.0 1.4 %copy-start = (bf16[6144,128]{1,0:T(8,128)(2,1)S(1)}, bf16[6144,128]{1,0:T(8,128)(2,1)}, u32[]{:S(2)}) copy-start(bf16[6144,128]{1,0:T(8,128)(2,1)} %rows_hbm.1) | copy-start | bytes 4718596
  1.4 0.7 copy-start.1
  2.1 0.7 copy-start.2
  2.7 0.7 copy-start.3
